TPU v7x, 32 devices: a whole 2x2x4 slice. The times are simulated.
32 devices in a mesh: groups: 2 (over x), section: 8 (over z, y), rows: 2 (over core).
Axes of the slice: x: 2, y: 2, z: 4, core: 2. Of those that a mesh axis runs over, the one named last changes fastest.
Arguments:
- inputs: bfloat16 [8, 16, 64, 256], P('groups', 'rows'), parts along dimension 0, may hold values from -6 to 6
- weights: bfloat16 [8, 2304, 256], P('section'), may hold values from -0.1875 to 0.1875
- cotangent: bfloat16 [8, 16, 64, 256], P('groups', 'rows'), parts along dimension 0, may hold values from -6 to 6
Outputs:
- section_outputs: bfloat16 [8, 8, 16, 64, 256], P('section', 'groups', 'rows'), parts along dimension 1
- grad_inputs: bfloat16 [8, 8, 16, 64, 256], P('section', 'groups', 'rows'), parts along dimension 1
- weight_grads: float32 [8, 4608, 256], P('section', 'groups'), parts along dimension 1
There are 2 independent parts, one for each index of `groups`. A program takes and returns all parts, laid end to end along the dimension named above; an argument that names none is the same for every part. Nothing has to cross between parts.
All inputs are finite; a program needn't handle non-finite values.
Results may differ from a plain program's by a relative error of at most 0.028.
Values may be sent and summed in bfloat16 or wider, within the bound.
A program may use at most 64 MiB of HBM per device.

v0:
```python
import math

import jax
import jax.numpy as jnp
from jax import lax
from jax.sharding import PartitionSpec as P

tanh_scale = 0.7978845608028654
cubic_term = 0.044715


def with_halo(x, sides, width):
    for axis, dim in sides:
        size, length = (lax.axis_size(axis), x.shape[dim])
        up = [(i, (i + 1) % size) for i in range(size - 1)]
        down = [(j, i) for i, j in up]
        last = lax.slice_in_dim(x, length - width, length, axis=dim)
        initial = lax.slice_in_dim(x, 0, width, axis=dim)
        before = lax.ppermute(last, axis, up)
        after = lax.ppermute(initial, axis, down)
        x = jnp.concatenate([before, x, after], axis=dim)
    return x


def shifted(block, axis, distance):
    devices = range(lax.axis_size(axis))
    route = [(i - distance, i) for i in devices if i - distance in devices]
    return lax.ppermute(block, axis, route)


def gelu_value(values):
    curved = jnp.tanh(tanh_scale * (values + cubic_term * values * values * values))
    return 0.5 * values * (1.0 + curved)


def gelu_slope(values):
    curved = jnp.tanh(tanh_scale * (values + cubic_term * values * values * values))
    return 0.5 * (1.0 + curved) + 0.5 * values * (1.0 - curved * curved) * tanh_scale * (
        1.0 + 3.0 * cubic_term * values * values
    )


def window(padded, row_count, col_count):
    return jnp.concatenate(
        [
            padded[row_off : row_off + row_count, col_off : col_off + col_count]
            for row_off in range(3)
            for col_off in range(3)
        ],
        axis=-1,
    )


def flipped(padded, row_count, col_count):
    return jnp.concatenate(
        [
            padded[2 - row_off : 2 - row_off + row_count, 2 - col_off : 2 - col_off + col_count]
            for row_off in range(3)
            for col_off in range(3)
        ],
        axis=-1,
    )


def on_device(inputs, weights, cotangent):
    kernel = weights[0]
    channels = kernel.shape[1]
    transposed = (
        kernel.reshape(9, channels, channels).transpose(0, 2, 1).reshape(9 * channels, channels)
    )
    micro_count = inputs.shape[0]
    row_count = inputs.shape[1]
    col_count = inputs.shape[2]
    pixels = row_count * col_count
    section_count = lax.axis_size("section")
    section_pos = lax.axis_index("section")
    tick_count = micro_count + section_count - 1
    empty_act = jnp.zeros((row_count, col_count, channels), jnp.bfloat16)
    arriving = empty_act
    saved_inputs = jnp.zeros((micro_count, row_count + 2, col_count + 2, channels), jnp.bfloat16)
    saved_preact = jnp.zeros((micro_count, row_count, col_count, channels), jnp.float32)
    saved_outputs = jnp.zeros((micro_count, row_count, col_count, channels), jnp.bfloat16)

    def forward_tick(moment, state_in):
        arriving, kept_inputs, kept_preact, kept_outputs = state_in
        micro_slot = moment - section_pos
        active = jnp.logical_and(micro_slot >= 0, micro_slot < micro_count)
        clamped = jnp.clip(micro_slot, 0, micro_count - 1)
        source = lax.dynamic_index_in_dim(inputs, clamped, 0, keepdims=False)
        current = jnp.where(section_pos == 0, source, arriving)
        rimmed = with_halo(current, (("rows", 0),), 1)
        framed = jnp.pad(rimmed, ((0, 0), (1, 1), (0, 0)))

        def advance(stored):
            stored_inputs, stored_preact, stored_outputs = stored
            preact = jnp.dot(
                window(framed, row_count, col_count).reshape(pixels, 9 * channels),
                kernel,
                preferred_element_type=jnp.float32,
            ).reshape(row_count, col_count, channels)
            result = gelu_value(preact).astype(jnp.bfloat16)
            stored_inputs = lax.dynamic_update_index_in_dim(stored_inputs, framed, clamped, 0)
            stored_preact = lax.dynamic_update_index_in_dim(stored_preact, preact, clamped, 0)
            stored_outputs = lax.dynamic_update_index_in_dim(stored_outputs, result, clamped, 0)
            return (result, (stored_inputs, stored_preact, stored_outputs))

        def resting(stored):
            return (empty_act, stored)

        result, stored = lax.cond(
            active, advance, resting, (kept_inputs, kept_preact, kept_outputs)
        )
        outgoing = shifted(result, "section", 1)
        return (outgoing,) + stored

    arriving, saved_inputs, saved_preact, saved_outputs = lax.fori_loop(
        0, tick_count, forward_tick, (arriving, saved_inputs, saved_preact, saved_outputs)
    )
    saved_grads = jnp.zeros((micro_count, row_count, col_count, channels), jnp.bfloat16)
    grad_start = jnp.zeros((9 * channels, channels), jnp.float32)
    zero_term = jnp.zeros((9 * channels, channels), jnp.float32)

    def backward_tick(moment, state_in):
        arriving, kept_grads, grad_total = state_in
        micro_slot = moment - (section_count - 1 - section_pos)
        active = jnp.logical_and(micro_slot >= 0, micro_slot < micro_count)
        clamped = jnp.clip(micro_slot, 0, micro_count - 1)
        source = lax.dynamic_index_in_dim(cotangent, clamped, 0, keepdims=False)
        upstream = jnp.where(section_pos == section_count - 1, source, arriving)
        preact = lax.dynamic_index_in_dim(saved_preact, clamped, 0, keepdims=False)
        local_grad = lax.cond(
            active,
            lambda: (upstream.astype(jnp.float32) * gelu_slope(preact)).astype(jnp.bfloat16),
            lambda: empty_act,
        )
        rimmed = with_halo(local_grad, (("rows", 0),), 1)
        padded_grad = jnp.pad(rimmed, ((0, 0), (1, 1), (0, 0)))
        stored_in = lax.dynamic_index_in_dim(saved_inputs, clamped, 0, keepdims=False)

        def input_grad():
            return (
                jnp.dot(
                    flipped(padded_grad, row_count, col_count).reshape(pixels, 9 * channels),
                    transposed,
                    preferred_element_type=jnp.float32,
                )
                .reshape(row_count, col_count, channels)
                .astype(jnp.bfloat16)
            )

        def weight_term():
            columns = window(stored_in, row_count, col_count).reshape(pixels, 9 * channels)
            return lax.dot_general(
                columns,
                local_grad.reshape(pixels, channels),
                (((0,), (0,)), ((), ())),
                preferred_element_type=jnp.float32,
            )

        passed, increment = lax.cond(
            active, lambda: (input_grad(), weight_term()), lambda: (empty_act, zero_term)
        )
        grad_total = grad_total + increment
        outgoing = shifted(passed, "section", -1)
        previous = lax.dynamic_index_in_dim(kept_grads, clamped, 0, keepdims=False)
        kept_grads = lax.dynamic_update_index_in_dim(
            kept_grads, jnp.where(active, passed, previous), clamped, 0
        )
        return (outgoing, kept_grads, grad_total)

    arriving_grad = empty_act
    arriving_grad, saved_grads, grad_total = lax.fori_loop(
        0, tick_count, backward_tick, (arriving_grad, saved_grads, grad_start)
    )
    summed = lax.psum(grad_total.astype(jnp.bfloat16), "rows").astype(jnp.float32)
    factor = 1.0 / math.sqrt(micro_count * row_count * lax.axis_size("rows") * col_count)
    return (saved_outputs[None], saved_grads[None], (summed * factor)[None])


def solution(mesh):
    placed = (
        P("groups", "rows", None, None),
        P("section", None, None),
        P("groups", "rows", None, None),
    )
    return jax.shard_map(
        on_device,
        mesh=mesh,
        in_specs=placed,
        out_specs=(
            P("section", "groups", "rows", None, None),
            P("section", "groups", "rows", None, None),
            P("section", "groups", None),
        ),
        check_vma=False,
    )
```

profile of v0, /device:TPU:1, one launch (start us, length us, event | category | flops | bytes accessed | tf_op | source)
XLA Modules:
  0.0 509.1 jit_solution(9154361861760113763)
XLA Ops:
  13.6 210.2 %while.41 = (s32[]{:T(128)}, bf16[8,64,256]{2,1,0:T(8,128)(2,1)S(1)}, bf16[4,10,66,256]{3,2,1,0:T(8,128)(2,1)}, f32[4,8,64,256]{3,2,1,0:T(8,128)}, bf16[4,8,64,2...) while((s32[]{:T(128)}, ...), condition=%wide.region_3.4_spmd, body=%wide.region_0.3_spmd.sunk | while | flops 606797824 | bytes 15376846 | solution.py:116
  25.0 5.7 %collective-permute-done.2 = bf16[8,64,256]{2,1,0:T(8,128)(2,1)S(1)} collective-permute-done((bf16[8,64,256]{2,1,0:T(8,128)(2,1)S(1)}, bf16[8,64,256]{2,1,0:T(8,128)(2,1)S(1)}, u32[]{:S(2)}, u32[]{:S(2)}) %collective-permute-start.2) | collective-permute-done | bytes 262176 | tf_op jit(solution)/shard_map/while/body/eval_jaxpr/ppermute | solution.py:28
  45.8 5.5 %collective-permute-done.2 = bf16[8,64,256]{2,1,0:T(8,128)(2,1)S(1)} collective-permute-done((bf16[8,64,256]{2,1,0:T(8,128)(2,1)S(1)}, bf16[8,64,256]{2,1,0:T(8,128)(2,1)S(1)}, u32[]{:S(2)}, u32[]{:S(2)}) %collective-permute-start.2) | collective-permute-done | bytes 262176 | tf_op jit(solution)/shard_map/while/body/eval_jaxpr/ppermute | solution.py:28
  66.5 5.5 %collective-permute-done.2 = bf16[8,64,256]{2,1,0:T(8,128)(2,1)S(1)} collective-permute-done((bf16[8,64,256]{2,1,0:T(8,128)(2,1)S(1)}, bf16[8,64,256]{2,1,0:T(8,128)(2,1)S(1)}, u32[]{:S(2)}, u32[]{:S(2)}) %collective-permute-start.2) | collective-permute-done | bytes 262176 | tf_op jit(solution)/shard_map/while/body/eval_jaxpr/ppermute | solution.py:28
  87.2 5.5 %collective-permute-done.2 = bf16[8,64,256]{2,1,0:T(8,128)(2,1)S(1)} collective-permute-done((bf16[8,64,256]{2,1,0:T(8,128)(2,1)S(1)}, bf16[8,64,256]{2,1,0:T(8,128)(2,1)S(1)}, u32[]{:S(2)}, u32[]{:S(2)}) %collective-permute-start.2) | collective-permute-done | bytes 262176 | tf_op jit(solution)/shard_map/while/body/eval_jaxpr/ppermute | solution.py:28
  99.8 8.1 %collective-permute-start.2 = (bf16[8,64,256]{2,1,0:T(8,128)(2,1)S(1)}, bf16[8,64,256]{2,1,0:T(8,128)(2,1)S(1)}, u32[]{:S(2)}, u32[]{:S(2)}) collective-permute-start(bf16[8,64,256]{2,1,0:T(8,128)(2,1)S(1)} %get-tuple-element.800), channel_id=1, source_target_pairs={{0,2},{2,4},{4,6},{6,8},{8,10},{10,12},{12,14},{1,3},{3,5},{5,7},{... | collective-permute-start | bytes 786440 | tf_op jit(solution)/shard_map/while/body/eval_jaxpr/ppermute | solution.py:28
  107.9 5.5 %collective-permute-done.2 = bf16[8,64,256]{2,1,0:T(8,128)(2,1)S(1)} collective-permute-done((bf16[8,64,256]{2,1,0:T(8,128)(2,1)S(1)}, bf16[8,64,256]{2,1,0:T(8,128)(2,1)S(1)}, u32[]{:S(2)}, u32[]{:S(2)}) %collective-permute-start.2) | collective-permute-done | bytes 262176 | tf_op jit(solution)/shard_map/while/body/eval_jaxpr/ppermute | solution.py:28
  120.5 4.6 collective-permute-start.2
  125.1 5.5 %collective-permute-done.2 = bf16[8,64,256]{2,1,0:T(8,128)(2,1)S(1)} collective-permute-done((bf16[8,64,256]{2,1,0:T(8,128)(2,1)S(1)}, bf16[8,64,256]{2,1,0:T(8,128)(2,1)S(1)}, u32[]{:S(2)}, u32[]{:S(2)}) %collective-permute-start.2) | collective-permute-done | bytes 262176 | tf_op jit(solution)/shard_map/while/body/eval_jaxpr/ppermute | solution.py:28
  137.7 9.0 %collective-permute-start.2 = (bf16[8,64,256]{2,1,0:T(8,128)(2,1)S(1)}, bf16[8,64,256]{2,1,0:T(8,128)(2,1)S(1)}, u32[]{:S(2)}, u32[]{:S(2)}) collective-permute-start(bf16[8,64,256]{2,1,0:T(8,128)(2,1)S(1)} %get-tuple-element.800), channel_id=1, source_target_pairs={{0,2},{2,4},{4,6},{6,8},{8,10},{10,12},{12,14},{1,3},{3,5},{5,7},{... | collective-permute-start | bytes 786440 | tf_op jit(solution)/shard_map/while/body/eval_jaxpr/ppermute | solution.py:28
  146.8 5.5 %collective-permute-done.2 = bf16[8,64,256]{2,1,0:T(8,128)(2,1)S(1)} collective-permute-done((bf16[8,64,256]{2,1,0:T(8,128)(2,1)S(1)}, bf16[8,64,256]{2,1,0:T(8,128)(2,1)S(1)}, u32[]{:S(2)}, u32[]{:S(2)}) %collective-permute-start.2) | collective-permute-done | bytes 262176 | tf_op jit(solution)/shard_map/while/body/eval_jaxpr/ppermute | solution.py:28
  159.4 5.0 collective-permute-start.2
  164.4 5.5 %collective-permute-done.2 = bf16[8,64,256]{2,1,0:T(8,128)(2,1)S(1)} collective-permute-done((bf16[8,64,256]{2,1,0:T(8,128)(2,1)S(1)}, bf16[8,64,256]{2,1,0:T(8,128)(2,1)S(1)}, u32[]{:S(2)}, u32[]{:S(2)}) %collective-permute-start.2) | collective-permute-done | bytes 262176 | tf_op jit(solution)/shard_map/while/body/eval_jaxpr/ppermute | solution.py:28
  177.0 5.0 collective-permute-start.2
  182.1 5.5 %collective-permute-done.2 = bf16[8,64,256]{2,1,0:T(8,128)(2,1)S(1)} collective-permute-done((bf16[8,64,256]{2,1,0:T(8,128)(2,1)S(1)}, bf16[8,64,256]{2,1,0:T(8,128)(2,1)S(1)}, u32[]{:S(2)}, u32[]{:S(2)}) %collective-permute-start.2) | collective-permute-done | bytes 262176 | tf_op jit(solution)/shard_map/while/body/eval_jaxpr/ppermute | solution.py:28
  194.7 5.0 collective-permute-start.2
  199.7 5.5 %collective-permute-done.2 = bf16[8,64,256]{2,1,0:T(8,128)(2,1)S(1)} collective-permute-done((bf16[8,64,256]{2,1,0:T(8,128)(2,1)S(1)}, bf16[8,64,256]{2,1,0:T(8,128)(2,1)S(1)}, u32[]{:S(2)}, u32[]{:S(2)}) %collective-permute-start.2) | collective-permute-done | bytes 262176 | tf_op jit(solution)/shard_map/while/body/eval_jaxpr/ppermute | solution.py:28
  212.3 5.9 %collective-permute-start.2 = (bf16[8,64,256]{2,1,0:T(8,128)(2,1)S(1)}, bf16[8,64,256]{2,1,0:T(8,128)(2,1)S(1)}, u32[]{:S(2)}, u32[]{:S(2)}) collective-permute-start(bf16[8,64,256]{2,1,0:T(8,128)(2,1)S(1)} %get-tuple-element.800), channel_id=1, source_target_pairs={{0,2},{2,4},{4,6},{6,8},{8,10},{10,12},{12,14},{1,3},{3,5},{5,7},{... | collective-permute-start | bytes 786440 | tf_op jit(solution)/shard_map/while/body/eval_jaxpr/ppermute | solution.py:28
  218.2 5.5 %collective-permute-done.2 = bf16[8,64,256]{2,1,0:T(8,128)(2,1)S(1)} collective-permute-done((bf16[8,64,256]{2,1,0:T(8,128)(2,1)S(1)}, bf16[8,64,256]{2,1,0:T(8,128)(2,1)S(1)}, u32[]{:S(2)}, u32[]{:S(2)}) %collective-permute-start.2) | collective-permute-done | bytes 262176 | tf_op jit(solution)/shard_map/while/body/eval_jaxpr/ppermute | solution.py:28
  224.9 252.2 %while.42 = (s32[]{:T(128)}, bf16[8,64,256]{2,1,0:T(8,128)(2,1)S(1)}, bf16[4,8,64,256]{3,2,1,0:T(8,128)(2,1)}, f32[2304,256]{1,0:T(8,128)}, s32[]{:T(128)}, /*in...) while((s32[]{:T(128)}, ...), condition=%wide.region_9.10_spmd.clone, body=%wide.region_4.9_spmd.clone.sunk | while | flops 1212481536 | bytes 35804116 | solution.py:172
  234.9 7.6 %collective-permute-done.5 = bf16[8,64,256]{2,1,0:T(8,128)(2,1)S(1)} collective-permute-done((bf16[8,64,256]{2,1,0:T(8,128)(2,1)S(1)}, bf16[8,64,256]{2,1,0:T(8,128)(2,1)S(1)}, u32[]{:S(2)}, u32[]{:S(2)}) %collective-permute-start.5) | collective-permute-done | bytes 262176 | tf_op jit(solution)/shard_map/while/body/eval_jaxpr/ppermute | solution.py:28
  254.2 6.0 %collective-permute-done.5 = bf16[8,64,256]{2,1,0:T(8,128)(2,1)S(1)} collective-permute-done((bf16[8,64,256]{2,1,0:T(8,128)(2,1)S(1)}, bf16[8,64,256]{2,1,0:T(8,128)(2,1)S(1)}, u32[]{:S(2)}, u32[]{:S(2)}) %collective-permute-start.5) | collective-permute-done | bytes 262176 | tf_op jit(solution)/shard_map/while/body/eval_jaxpr/ppermute | solution.py:28
  271.8 6.0 %collective-permute-done.5 = bf16[8,64,256]{2,1,0:T(8,128)(2,1)S(1)} collective-permute-done((bf16[8,64,256]{2,1,0:T(8,128)(2,1)S(1)}, bf16[8,64,256]{2,1,0:T(8,128)(2,1)S(1)}, u32[]{:S(2)}, u32[]{:S(2)}) %collective-permute-start.5) | collective-permute-done | bytes 262176 | tf_op jit(solution)/shard_map/while/body/eval_jaxpr/ppermute | solution.py:28
  289.4 6.9 %collective-permute-done.5 = bf16[8,64,256]{2,1,0:T(8,128)(2,1)S(1)} collective-permute-done((bf16[8,64,256]{2,1,0:T(8,128)(2,1)S(1)}, bf16[8,64,256]{2,1,0:T(8,128)(2,1)S(1)}, u32[]{:S(2)}, u32[]{:S(2)}) %collective-permute-start.5) | collective-permute-done | bytes 262176 | tf_op jit(solution)/shard_map/while/body/eval_jaxpr/ppermute | solution.py:28
  307.9 6.0 %collective-permute-done.5 = bf16[8,64,256]{2,1,0:T(8,128)(2,1)S(1)} collective-permute-done((bf16[8,64,256]{2,1,0:T(8,128)(2,1)S(1)}, bf16[8,64,256]{2,1,0:T(8,128)(2,1)S(1)}, u32[]{:S(2)}, u32[]{:S(2)}) %collective-permute-start.5) | collective-permute-done | bytes 262176 | tf_op jit(solution)/shard_map/while/body/eval_jaxpr/ppermute | solution.py:28
  325.4 6.0 %collective-permute-done.5 = bf16[8,64,256]{2,1,0:T(8,128)(2,1)S(1)} collective-permute-done((bf16[8,64,256]{2,1,0:T(8,128)(2,1)S(1)}, bf16[8,64,256]{2,1,0:T(8,128)(2,1)S(1)}, u32[]{:S(2)}, u32[]{:S(2)}) %collective-permute-start.5) | collective-permute-done | bytes 262176 | tf_op jit(solution)/shard_map/while/body/eval_jaxpr/ppermute | solution.py:28
  343.0 44.8 %collective-permute-done.5 = bf16[8,64,256]{2,1,0:T(8,128)(2,1)S(1)} collective-permute-done((bf16[8,64,256]{2,1,0:T(8,128)(2,1)S(1)}, bf16[8,64,256]{2,1,0:T(8,128)(2,1)S(1)}, u32[]{:S(2)}, u32[]{:S(2)}) %collective-permute-start.5) | collective-permute-done | bytes 262176 | tf_op jit(solution)/shard_map/while/body/eval_jaxpr/ppermute | solution.py:28
  395.3 4.5 conditional.10
  405.2 5.2 %collective-permute-done.5 = bf16[8,64,256]{2,1,0:T(8,128)(2,1)S(1)} collective-permute-done((bf16[8,64,256]{2,1,0:T(8,128)(2,1)S(1)}, bf16[8,64,256]{2,1,0:T(8,128)(2,1)S(1)}, u32[]{:S(2)}, u32[]{:S(2)}) %collective-permute-start.5) | collective-permute-done | bytes 262176 | tf_op jit(solution)/shard_map/while/body/eval_jaxpr/ppermute | solution.py:28
  427.8 5.2 %collective-permute-done.5 = bf16[8,64,256]{2,1,0:T(8,128)(2,1)S(1)} collective-permute-done((bf16[8,64,256]{2,1,0:T(8,128)(2,1)S(1)}, bf16[8,64,256]{2,1,0:T(8,128)(2,1)S(1)}, u32[]{:S(2)}, u32[]{:S(2)}) %collective-permute-start.5) | collective-permute-done | bytes 262176 | tf_op jit(solution)/shard_map/while/body/eval_jaxpr/ppermute | solution.py:28
  450.4 5.2 %collective-permute-done.5 = bf16[8,64,256]{2,1,0:T(8,128)(2,1)S(1)} collective-permute-done((bf16[8,64,256]{2,1,0:T(8,128)(2,1)S(1)}, bf16[8,64,256]{2,1,0:T(8,128)(2,1)S(1)}, u32[]{:S(2)}, u32[]{:S(2)}) %collective-permute-start.5) | collective-permute-done | bytes 262176 | tf_op jit(solution)/shard_map/while/body/eval_jaxpr/ppermute | solution.py:28
  479.9 19.5 %all-reduce.4.cloned.1.call-done = bf16[2304,256]{1,0:T(8,128)(2,1)} async-done(((bf16[2304,256]{1,0:T(8,128)(2,1)}), bf16[2304,256]{1,0:T(8,128)(2,1)}) %all-reduce.4.cloned.1.call-update) | async-done | bytes 1179664 | tf_op jit(solution)/shard_map/psum | solution.py:175
  (418 shorter events, 307.6 us)
Async XLA Ops:
  7.2 492.2 %all-reduce.4.cloned.1.call-start = ((), (), s32[]{:S(2)}) async-start(), calls=%async_computation | async-start | bytes 2359296 | tf_op jit(solution)/shard_map/psum | solution.py:175
  23.7 7.0 %collective-permute-start.2 = (bf16[8,64,256]{2,1,0:T(8,128)(2,1)S(1)}, bf16[8,64,256]{2,1,0:T(8,128)(2,1)S(1)}, u32[]{:S(2)}, u32[]{:S(2)}) collective-permute-start(bf16[8,64,256]{2,1,0:T(8,128)(2,1)S(1)} %get-tuple-element.800), channel_id=1, source_target_pairs={{0,2},{2,4},{4,6},{6,8},{8,10},{10,12},{12,14},{1,3},{3,5},{5,7},{... | collective-permute-start | bytes 786440 | tf_op jit(solution)/shard_map/while/body/eval_jaxpr/ppermute | solution.py:28
  41.6 9.6 %collective-permute-start.2 = (bf16[8,64,256]{2,1,0:T(8,128)(2,1)S(1)}, bf16[8,64,256]{2,1,0:T(8,128)(2,1)S(1)}, u32[]{:S(2)}, u32[]{:S(2)}) collective-permute-start(bf16[8,64,256]{2,1,0:T(8,128)(2,1)S(1)} %get-tuple-element.800), channel_id=1, source_target_pairs={{0,2},{2,4},{4,6},{6,8},{8,10},{10,12},{12,14},{1,3},{3,5},{5,7},{... | collective-permute-start | bytes 786440 | tf_op jit(solution)/shard_map/while/body/eval_jaxpr/ppermute | solution.py:28
  62.4 9.6 %collective-permute-start.2 = (bf16[8,64,256]{2,1,0:T(8,128)(2,1)S(1)}, bf16[8,64,256]{2,1,0:T(8,128)(2,1)S(1)}, u32[]{:S(2)}, u32[]{:S(2)}) collective-permute-start(bf16[8,64,256]{2,1,0:T(8,128)(2,1)S(1)} %get-tuple-element.800), channel_id=1, source_target_pairs={{0,2},{2,4},{4,6},{6,8},{8,10},{10,12},{12,14},{1,3},{3,5},{5,7},{... | collective-permute-start | bytes 786440 | tf_op jit(solution)/shard_map/while/body/eval_jaxpr/ppermute | solution.py:28
  83.1 9.6 %collective-permute-start.2 = (bf16[8,64,256]{2,1,0:T(8,128)(2,1)S(1)}, bf16[8,64,256]{2,1,0:T(8,128)(2,1)S(1)}, u32[]{:S(2)}, u32[]{:S(2)}) collective-permute-start(bf16[8,64,256]{2,1,0:T(8,128)(2,1)S(1)} %get-tuple-element.800), channel_id=1, source_target_pairs={{0,2},{2,4},{4,6},{6,8},{8,10},{10,12},{12,14},{1,3},{3,5},{5,7},{... | collective-permute-start | bytes 786440 | tf_op jit(solution)/shard_map/while/body/eval_jaxpr/ppermute | solution.py:28
  99.8 13.7 %collective-permute-start.2 = (bf16[8,64,256]{2,1,0:T(8,128)(2,1)S(1)}, bf16[8,64,256]{2,1,0:T(8,128)(2,1)S(1)}, u32[]{:S(2)}, u32[]{:S(2)}) collective-permute-start(bf16[8,64,256]{2,1,0:T(8,128)(2,1)S(1)} %get-tuple-element.800), channel_id=1, source_target_pairs={{0,2},{2,4},{4,6},{6,8},{8,10},{10,12},{12,14},{1,3},{3,5},{5,7},{... | collective-permute-start | bytes 786440 | tf_op jit(solution)/shard_map/while/body/eval_jaxpr/ppermute | solution.py:28
  120.5 10.1 %collective-permute-start.2 = (bf16[8,64,256]{2,1,0:T(8,128)(2,1)S(1)}, bf16[8,64,256]{2,1,0:T(8,128)(2,1)S(1)}, u32[]{:S(2)}, u32[]{:S(2)}) collective-permute-start(bf16[8,64,256]{2,1,0:T(8,128)(2,1)S(1)} %get-tuple-element.800), channel_id=1, source_target_pairs={{0,2},{2,4},{4,6},{6,8},{8,10},{10,12},{12,14},{1,3},{3,5},{5,7},{... | collective-permute-start | bytes 786440 | tf_op jit(solution)/shard_map/while/body/eval_jaxpr/ppermute | solution.py:28
  137.7 14.6 %collective-permute-start.2 = (bf16[8,64,256]{2,1,0:T(8,128)(2,1)S(1)}, bf16[8,64,256]{2,1,0:T(8,128)(2,1)S(1)}, u32[]{:S(2)}, u32[]{:S(2)}) collective-permute-start(bf16[8,64,256]{2,1,0:T(8,128)(2,1)S(1)} %get-tuple-element.800), channel_id=1, source_target_pairs={{0,2},{2,4},{4,6},{6,8},{8,10},{10,12},{12,14},{1,3},{3,5},{5,7},{... | collective-permute-start | bytes 786440 | tf_op jit(solution)/shard_map/while/body/eval_jaxpr/ppermute | solution.py:28
  159.4 10.6 %collective-permute-start.2 = (bf16[8,64,256]{2,1,0:T(8,128)(2,1)S(1)}, bf16[8,64,256]{2,1,0:T(8,128)(2,1)S(1)}, u32[]{:S(2)}, u32[]{:S(2)}) collective-permute-start(bf16[8,64,256]{2,1,0:T(8,128)(2,1)S(1)} %get-tuple-element.800), channel_id=1, source_target_pairs={{0,2},{2,4},{4,6},{6,8},{8,10},{10,12},{12,14},{1,3},{3,5},{5,7},{... | collective-permute-start | bytes 786440 | tf_op jit(solution)/shard_map/while/body/eval_jaxpr/ppermute | solution.py:28
  177.0 10.6 %collective-permute-start.2 = (bf16[8,64,256]{2,1,0:T(8,128)(2,1)S(1)}, bf16[8,64,256]{2,1,0:T(8,128)(2,1)S(1)}, u32[]{:S(2)}, u32[]{:S(2)}) collective-permute-start(bf16[8,64,256]{2,1,0:T(8,128)(2,1)S(1)} %get-tuple-element.800), channel_id=1, source_target_pairs={{0,2},{2,4},{4,6},{6,8},{8,10},{10,12},{12,14},{1,3},{3,5},{5,7},{... | collective-permute-start | bytes 786440 | tf_op jit(solution)/shard_map/while/body/eval_jaxpr/ppermute | solution.py:28
  194.7 10.6 %collective-permute-start.2 = (bf16[8,64,256]{2,1,0:T(8,128)(2,1)S(1)}, bf16[8,64,256]{2,1,0:T(8,128)(2,1)S(1)}, u32[]{:S(2)}, u32[]{:S(2)}) collective-permute-start(bf16[8,64,256]{2,1,0:T(8,128)(2,1)S(1)} %get-tuple-element.800), channel_id=1, source_target_pairs={{0,2},{2,4},{4,6},{6,8},{8,10},{10,12},{12,14},{1,3},{3,5},{5,7},{... | collective-permute-start | bytes 786440 | tf_op jit(solution)/shard_map/while/body/eval_jaxpr/ppermute | solution.py:28
  212.3 11.5 %collective-permute-start.2 = (bf16[8,64,256]{2,1,0:T(8,128)(2,1)S(1)}, bf16[8,64,256]{2,1,0:T(8,128)(2,1)S(1)}, u32[]{:S(2)}, u32[]{:S(2)}) collective-permute-start(bf16[8,64,256]{2,1,0:T(8,128)(2,1)S(1)} %get-tuple-element.800), channel_id=1, source_target_pairs={{0,2},{2,4},{4,6},{6,8},{8,10},{10,12},{12,14},{1,3},{3,5},{5,7},{... | collective-permute-start | bytes 786440 | tf_op jit(solution)/shard_map/while/body/eval_jaxpr/ppermute | solution.py:28
  224.9 5.2 %collective-permute-start.3 = (bf16[1,64,256]{2,1,0:T(8,128)(2,1)S(1)}, bf16[1,64,256]{2,1,0:T(8,128)(2,1)S(1)}, u32[]{:S(2)}, u32[]{:S(2)}) collective-permute-start(bf16[1,64,256]{2,1,0:T(8,128)(2,1)S(1)} %get-tuple-element.814), channel_id=1, source_target_pairs={{1,0},{3,2},{5,4},{7,6},{9,8},{11,10},{13,12},{15,14},{17,16},{19,... | collective-permute-start | bytes 98312 | tf_op jit(solution)/shard_map/while/body/eval_jaxpr/ppermute | solution.py:20
  231.2 11.4 %collective-permute-start.5 = (bf16[8,64,256]{2,1,0:T(8,128)(2,1)S(1)}, bf16[8,64,256]{2,1,0:T(8,128)(2,1)S(1)}, u32[]{:S(2)}, u32[]{:S(2)}) collective-permute-start(bf16[8,64,256]{2,1,0:T(8,128)(2,1)S(1)} %get-tuple-element.816), channel_id=1, source_target_pairs={{2,0},{4,2},{6,4},{8,6},{10,8},{12,10},{14,12},{3,1},{5,3},{7,5},{... | collective-permute-start | bytes 786440 | tf_op jit(solution)/shard_map/while/body/eval_jaxpr/ppermute | solution.py:28
  242.6 5.0 collective-permute-start.3
  248.7 11.4 %collective-permute-start.5 = (bf16[8,64,256]{2,1,0:T(8,128)(2,1)S(1)}, bf16[8,64,256]{2,1,0:T(8,128)(2,1)S(1)}, u32[]{:S(2)}, u32[]{:S(2)}) collective-permute-start(bf16[8,64,256]{2,1,0:T(8,128)(2,1)S(1)} %get-tuple-element.816), channel_id=1, source_target_pairs={{2,0},{4,2},{6,4},{8,6},{10,8},{12,10},{14,12},{3,1},{5,3},{7,5},{... | collective-permute-start | bytes 786440 | tf_op jit(solution)/shard_map/while/body/eval_jaxpr/ppermute | solution.py:28
  260.2 5.0 collective-permute-start.3
  266.3 11.4 %collective-permute-start.5 = (bf16[8,64,256]{2,1,0:T(8,128)(2,1)S(1)}, bf16[8,64,256]{2,1,0:T(8,128)(2,1)S(1)}, u32[]{:S(2)}, u32[]{:S(2)}) collective-permute-start(bf16[8,64,256]{2,1,0:T(8,128)(2,1)S(1)} %get-tuple-element.816), channel_id=1, source_target_pairs={{2,0},{4,2},{6,4},{8,6},{10,8},{12,10},{14,12},{3,1},{5,3},{7,5},{... | collective-permute-start | bytes 786440 | tf_op jit(solution)/shard_map/while/body/eval_jaxpr/ppermute | solution.py:28
  277.8 5.0 collective-permute-start.3
  283.9 12.3 %collective-permute-start.5 = (bf16[8,64,256]{2,1,0:T(8,128)(2,1)S(1)}, bf16[8,64,256]{2,1,0:T(8,128)(2,1)S(1)}, u32[]{:S(2)}, u32[]{:S(2)}) collective-permute-start(bf16[8,64,256]{2,1,0:T(8,128)(2,1)S(1)} %get-tuple-element.816), channel_id=1, source_target_pairs={{2,0},{4,2},{6,4},{8,6},{10,8},{12,10},{14,12},{3,1},{5,3},{7,5},{... | collective-permute-start | bytes 786440 | tf_op jit(solution)/shard_map/while/body/eval_jaxpr/ppermute | solution.py:28
  296.3 5.0 collective-permute-start.3
  302.4 11.4 %collective-permute-start.5 = (bf16[8,64,256]{2,1,0:T(8,128)(2,1)S(1)}, bf16[8,64,256]{2,1,0:T(8,128)(2,1)S(1)}, u32[]{:S(2)}, u32[]{:S(2)}) collective-permute-start(bf16[8,64,256]{2,1,0:T(8,128)(2,1)S(1)} %get-tuple-element.816), channel_id=1, source_target_pairs={{2,0},{4,2},{6,4},{8,6},{10,8},{12,10},{14,12},{3,1},{5,3},{7,5},{... | collective-permute-start | bytes 786440 | tf_op jit(solution)/shard_map/while/body/eval_jaxpr/ppermute | solution.py:28
  313.9 5.0 collective-permute-start.3
  320.0 11.4 %collective-permute-start.5 = (bf16[8,64,256]{2,1,0:T(8,128)(2,1)S(1)}, bf16[8,64,256]{2,1,0:T(8,128)(2,1)S(1)}, u32[]{:S(2)}, u32[]{:S(2)}) collective-permute-start(bf16[8,64,256]{2,1,0:T(8,128)(2,1)S(1)} %get-tuple-element.816), channel_id=1, source_target_pairs={{2,0},{4,2},{6,4},{8,6},{10,8},{12,10},{14,12},{3,1},{5,3},{7,5},{... | collective-permute-start | bytes 786440 | tf_op jit(solution)/shard_map/while/body/eval_jaxpr/ppermute | solution.py:28
  331.5 5.0 collective-permute-start.3
  337.6 50.3 %collective-permute-start.5 = (bf16[8,64,256]{2,1,0:T(8,128)(2,1)S(1)}, bf16[8,64,256]{2,1,0:T(8,128)(2,1)S(1)}, u32[]{:S(2)}, u32[]{:S(2)}) collective-permute-start(bf16[8,64,256]{2,1,0:T(8,128)(2,1)S(1)} %get-tuple-element.816), channel_id=1, source_target_pairs={{2,0},{4,2},{6,4},{8,6},{10,8},{12,10},{14,12},{3,1},{5,3},{7,5},{... | collective-permute-start | bytes 786440 | tf_op jit(solution)/shard_map/while/body/eval_jaxpr/ppermute | solution.py:28
  389.4 5.0 collective-permute-start.3
  399.8 10.7 %collective-permute-start.5 = (bf16[8,64,256]{2,1,0:T(8,128)(2,1)S(1)}, bf16[8,64,256]{2,1,0:T(8,128)(2,1)S(1)}, u32[]{:S(2)}, u32[]{:S(2)}) collective-permute-start(bf16[8,64,256]{2,1,0:T(8,128)(2,1)S(1)} %get-tuple-element.816), channel_id=1, source_target_pairs={{2,0},{4,2},{6,4},{8,6},{10,8},{12,10},{14,12},{3,1},{5,3},{7,5},{... | collective-permute-start | bytes 786440 | tf_op jit(solution)/shard_map/while/body/eval_jaxpr/ppermute | solution.py:28
  422.4 10.7 %collective-permute-start.5 = (bf16[8,64,256]{2,1,0:T(8,128)(2,1)S(1)}, bf16[8,64,256]{2,1,0:T(8,128)(2,1)S(1)}, u32[]{:S(2)}, u32[]{:S(2)}) collective-permute-start(bf16[8,64,256]{2,1,0:T(8,128)(2,1)S(1)} %get-tuple-element.816), channel_id=1, source_target_pairs={{2,0},{4,2},{6,4},{8,6},{10,8},{12,10},{14,12},{3,1},{5,3},{7,5},{... | collective-permute-start | bytes 786440 | tf_op jit(solution)/shard_map/while/body/eval_jaxpr/ppermute | solution.py:28
  445.0 10.7 %collective-permute-start.5 = (bf16[8,64,256]{2,1,0:T(8,128)(2,1)S(1)}, bf16[8,64,256]{2,1,0:T(8,128)(2,1)S(1)}, u32[]{:S(2)}, u32[]{:S(2)}) collective-permute-start(bf16[8,64,256]{2,1,0:T(8,128)(2,1)S(1)} %get-tuple-element.816), channel_id=1, source_target_pairs={{2,0},{4,2},{6,4},{8,6},{10,8},{12,10},{14,12},{3,1},{5,3},{7,5},{... | collective-permute-start | bytes 786440 | tf_op jit(solution)/shard_map/while/body/eval_jaxpr/ppermute | solution.py:28
  457.2 5.0 collective-permute-start.3
  467.6 9.5 %collective-permute-start.5 = (bf16[8,64,256]{2,1,0:T(8,128)(2,1)S(1)}, bf16[8,64,256]{2,1,0:T(8,128)(2,1)S(1)}, u32[]{:S(2)}, u32[]{:S(2)}) collective-permute-start(bf16[8,64,256]{2,1,0:T(8,128)(2,1)S(1)} %get-tuple-element.816), channel_id=1, source_target_pairs={{2,0},{4,2},{6,4},{8,6},{10,8},{12,10},{14,12},{3,1},{5,3},{7,5},{... | collective-permute-start | bytes 786440 | tf_op jit(solution)/shard_map/while/body/eval_jaxpr/ppermute | solution.py:28
  (40 other events, 132.3 us)
Sparse Core Ops, SparseCore 0:
  480.0 19.3 all-reduce.3
where the time goes:
time: 512 us; the launch traced here: 509 us
  waiting for transfers between devices  212 us (41%)
  starting transfers between devices  160 us (31%)
  other arithmetic  71.4 us (14%)
  local copies, waits for them, and re-layouts  39.4 us (8%)
  between operations  14.1 us (3%)
  matrix products  9.47 us (2%)
    ppermute x22, waiting for transfers between devices, shifted(): return lax.ppermute(block, axis, route)  164 us
    ppermute x22, starting transfers between devices, shifted(): return lax.ppermute(block, axis, route)  70.6 us
    ppermute x22, starting transfers between devices, with_halo(): after = lax.ppermute(initial, axis, down)  60.7 us
    add x11, other arithmetic, backward_tick(): grad_total = grad_total + increment  35.6 us
    ppermute x22, waiting for transfers between devices, with_halo(): before = lax.ppermute(last, axis, up)  28.5 us
    ppermute x22, starting transfers between devices, with_halo(): before = lax.ppermute(last, axis, up)  28.4 us
    psum x1, waiting for transfers between devices, on_device(): lax.psum(grad_total.astype(jnp.bfloat16), 'rows').astype(jnp.float32)  19.5 us
    select_n x11, other arithmetic, forward_tick(): current = jnp.where(section_pos == 0, source, arriving)  10.8 us
  transfers between devices with their start and end apart: 67, of which 45 were waited for; matrix products, arithmetic and copies ran while one was open for 11% of the time, Pallas kernels for 0%

commit v1 on v0

v1 whole, which is shorter than its diff:
```python
import functools
import math

import jax
import jax.numpy as jnp
from jax import lax
from jax.experimental import pallas as pl
from jax.experimental.pallas import tpu as pltpu
from jax.sharding import PartitionSpec as P

MESH = pl.DeviceIdType.MESH
tanh_scale = 0.7978845608028654
cubic_term = 0.044715


def column_shifts(values):
    rows, cols, channels = values.shape
    flat = values.reshape(rows * cols, channels)
    col = lax.broadcasted_iota(jnp.int32, flat.shape, 0) % cols
    left = jnp.where(col == 0, 0.0, pltpu.roll(flat, 1, 0))
    right = jnp.where(col == cols - 1, 0.0, pltpu.roll(flat, rows * cols - 1, 0))
    return (
        left.astype(jnp.bfloat16).reshape(values.shape),
        right.astype(jnp.bfloat16).reshape(values.shape),
    )


def kernel(
    section_count,
    factor,
    in_ref,
    w_ref,
    cot_ref,
    out_ref,
    grad_ref,
    wgrad_ref,
    x3,
    u,
    slope,
    g3,
    wt,
    acc,
    wsend,
    wrecv,
    send_f,
    recv_f,
    send_b,
    recv_b,
    send_i,
    send_c,
    send_s,
    recv_s,
    send_w,
    recv_w,
):
    micros, rows, cols, chans = in_ref.shape
    half = rows // 2
    mid = pl.ds(chans, chans)
    s = lax.axis_index("section")
    r = lax.axis_index("rows")
    other = 1 - r
    last = section_count - 1
    is_first = s == 0
    is_last = s == last

    edge = (1 - r) * (rows - 1)
    halo = (1 - r) * (rows + 1)
    other_halo = r * (rows + 1)

    barrier = pltpu.get_barrier_semaphore()
    pl.semaphore_signal(barrier, inc=1, device_id={"rows": other}, device_id_type=MESH)

    @pl.when(s > 0)
    def _():
        for core in range(2):
            pl.semaphore_signal(
                barrier, inc=1, device_id={"section": s - 1, "rows": core}, device_id_type=MESH
            )

    @pl.when(s < last)
    def _():
        for core in range(2):
            pl.semaphore_signal(
                barrier, inc=1, device_id={"section": s + 1, "rows": core}, device_id_type=MESH
            )

    peers = 1 + 2 * (s > 0).astype(jnp.int32) + 2 * (s < last).astype(jnp.int32)
    pl.semaphore_wait(barrier, peers)

    def first_halo(m, dst_row):
        return pltpu.make_async_remote_copy(
            src_ref=in_ref.at[m, pl.ds(edge, 1)],
            dst_ref=x3.at[m, pl.ds(dst_row, 1), :, mid],
            send_sem=send_i.at[m],
            recv_sem=recv_f.at[m, 2],
            device_id={"rows": other},
            device_id_type=MESH,
        )

    def last_halo(m, dst_row):
        return pltpu.make_async_remote_copy(
            src_ref=cot_ref.at[m, pl.ds(edge, 1)],
            dst_ref=u.at[m, pl.ds(dst_row, 1)],
            send_sem=send_c.at[m],
            recv_sem=recv_b.at[m, 2],
            device_id={"rows": other},
            device_id_type=MESH,
        )

    def slope_halo(m, dst_row):
        return pltpu.make_async_remote_copy(
            src_ref=slope.at[m, pl.ds(edge + 1, 1)],
            dst_ref=slope.at[m, pl.ds(dst_row, 1)],
            send_sem=send_s.at[m],
            recv_sem=recv_s.at[m],
            device_id={"rows": other},
            device_id_type=MESH,
        )

    starts = (r * half, half - r, edge, (1 - r) * (half + 1))
    counts = (half, 1, 1, half - 1)

    def forward_piece(m, p, halo_row):
        start, count = starts[p], counts[p]
        where = halo_row if p == 2 else start + 1
        return pltpu.make_async_remote_copy(
            src_ref=out_ref.at[m, pl.ds(start, count)],
            dst_ref=x3.at[m, pl.ds(where, count), :, mid],
            send_sem=send_f.at[m, p],
            recv_sem=recv_f.at[m, p],
            device_id={"section": jnp.minimum(s + 1, last), "rows": other if p == 2 else r},
            device_id_type=MESH,
        )

    def backward_piece(m, p, halo_row):
        start, count = starts[p], counts[p]
        where = halo_row if p == 2 else start + 1
        return pltpu.make_async_remote_copy(
            src_ref=grad_ref.at[m, pl.ds(start, count)],
            dst_ref=u.at[m, pl.ds(where, count)],
            send_sem=send_b.at[m, p],
            recv_sem=recv_b.at[m, p],
            device_id={"section": jnp.maximum(s - 1, 0), "rows": other if p == 2 else r},
            device_id_type=MESH,
        )

    @pl.when(is_first)
    def _():
        def start(m, carry):
            first_halo(m, other_halo).start()
            return carry

        lax.fori_loop(0, micros, start, 0)

    @pl.when(is_last)
    def _():
        def start(m, carry):
            last_halo(m, other_halo).start()
            u[m, pl.ds(1, rows)] = cot_ref[m]
            return carry

        lax.fori_loop(0, micros, start, 0)

    blank = jnp.zeros((1, cols, 3 * chans), jnp.bfloat16)

    def clear(m, carry):
        x3[m, pl.ds(other_halo, 1)] = blank
        return carry

    lax.fori_loop(0, micros, clear, 0)
    g3[pl.ds(other_halo, 1)] = blank

    def transpose_weights():
        for k in range(9):
            wt[pl.ds((8 - k) * chans, chans), :] = w_ref[pl.ds(k * chans, chans), :].T

    @pl.when(s > 0)
    def _():
        transpose_weights()

    new_starts = (1 + r * (half - 1), (1 - r) * (half + 2))
    new_counts = (half + 1, rows - half)
    half_starts = (r * half, (1 - r) * half)

    def conv(field, kern, start):
        total = None
        for a in range(3):
            part = jnp.dot(
                field[pl.ds(start + a, half)].reshape(half * cols, 3 * chans),
                kern[pl.ds(a * 3 * chans, 3 * chans), :],
                preferred_element_type=jnp.float32,
            )
            total = part if total is None else total + part
        return total

    def forward(m):
        @pl.when(is_first)
        def _():
            x3[m, pl.ds(1, rows), :, mid] = in_ref[m]

        for k in range(2):
            @pl.when(s > 0)
            def _():
                for p in ((0, 1), (3,))[k]:
                    forward_piece(m, p, halo).wait_recv()

            if k == 1:
                forward_piece(m, 2, halo).wait_recv()
            fresh = pl.ds(new_starts[k], new_counts[k])
            left, right = column_shifts(x3[m, fresh, :, mid].astype(jnp.float32))
            x3[m, fresh, :, pl.ds(0, chans)] = left
            x3[m, fresh, :, pl.ds(2 * chans, chans)] = right
            start = half_starts[k]
            pre = conv(x3.at[m], w_ref, start)
            curved = jnp.tanh(tanh_scale * (pre + cubic_term * pre * pre * pre))
            value = 0.5 * pre * (1.0 + curved)
            out_ref[m, pl.ds(start, half)] = value.astype(jnp.bfloat16).reshape(half, cols, chans)

            @pl.when(s < last)
            def _():
                for p in ((0,), (1, 2, 3))[k]:
                    forward_piece(m, p, other_halo).start()

            steep = 0.5 * (1.0 + curved) + 0.5 * pre * (1.0 - curved * curved) * tanh_scale * (
                1.0 + 3.0 * cubic_term * pre * pre
            )
            slope[m, pl.ds(start + 1, half)] = steep.reshape(half, cols, chans)
        slope_halo(m, other_halo).start()

    def kernel_term(m, a):
        return lax.dot_general(
            x3[m, pl.ds(a, rows)].reshape(rows * cols, 3 * chans),
            g3[pl.ds(1, rows), :, mid].reshape(rows * cols, chans),
            (((0,), (0,)), ((), ())),
            preferred_element_type=jnp.float32,
        )

    def backward(m):
        for k in range(2):
            @pl.when(s < last)
            def _():
                for p in ((0, 1), (3,))[k]:
                    backward_piece(m, p, halo).wait_recv()

            if k == 1:
                backward_piece(m, 2, halo).wait_recv()
                slope_halo(m, halo).wait_recv()
            fresh = pl.ds(new_starts[k], new_counts[k])
            local = (u[m, fresh].astype(jnp.float32) * slope[m, fresh]).astype(jnp.bfloat16)
            left, right = column_shifts(local.astype(jnp.float32))
            g3[fresh, :, pl.ds(0, chans)] = left
            g3[fresh, :, mid] = local
            g3[fresh, :, pl.ds(2 * chans, chans)] = right
            start = half_starts[k]
            passed = conv(g3, wt, start)
            grad_ref[m, pl.ds(start, half)] = passed.astype(jnp.bfloat16).reshape(half, cols, chans)

            @pl.when(s > 0)
            def _():
                for p in ((0,), (1, 2, 3))[k]:
                    backward_piece(m, p, other_halo).start()

        @pl.when(m == 0)
        def _():
            for a in range(3):
                acc[pl.ds(a * 3 * chans, 3 * chans), :] = kernel_term(m, a)

        @pl.when(jnp.logical_and(m > 0, m < micros - 1))
        def _():
            for a in range(3):
                acc[pl.ds(a * 3 * chans, 3 * chans), :] += kernel_term(m, a)

    def forward_step(m, carry):
        forward(m)

        @pl.when(is_last)
        def _():
            backward(m)

        return carry

    lax.fori_loop(0, micros, forward_step, 0)

    @pl.when(s == 0)
    def _():
        transpose_weights()

    def backward_step(m, carry):
        backward(m)
        return carry

    @pl.when(s < last)
    def _():
        lax.fori_loop(0, micros, backward_step, 0)

    def kernel_copy(a):
        block = pl.ds(a * 3 * chans, 3 * chans)
        return pltpu.make_async_remote_copy(
            src_ref=wsend.at[block],
            dst_ref=wrecv.at[block],
            send_sem=send_w.at[a],
            recv_sem=recv_w.at[a],
            device_id={"rows": other},
            device_id_type=MESH,
        )

    for a in range(3):
        block = pl.ds(a * 3 * chans, 3 * chans)
        term = kernel_term(micros - 1, a)
        total = term if micros == 1 else acc[block, :] + term
        wsend[block, :] = total.astype(jnp.bfloat16)
        kernel_copy(a).start()
    for a in range(3):
        block = pl.ds(a * 3 * chans, 3 * chans)
        kernel_copy(a).wait_recv()
        wgrad_ref[block, :] = (
            wsend[block, :].astype(jnp.float32) + wrecv[block, :].astype(jnp.float32)
        ) * factor

    def finish(m, carry):
        slope_halo(m, other_halo).wait_send()

        @pl.when(s < last)
        def _():
            for p in range(4):
                forward_piece(m, p, other_halo).wait_send()

        @pl.when(s > 0)
        def _():
            for p in range(4):
                backward_piece(m, p, other_halo).wait_send()

        @pl.when(is_first)
        def _():
            first_halo(m, other_halo).wait_send()

        @pl.when(is_last)
        def _():
            last_halo(m, other_halo).wait_send()

        return carry

    lax.fori_loop(0, micros, finish, 0)
    for a in range(3):
        kernel_copy(a).wait_send()


def on_device(inputs, weights, cotangent):
    micros, rows, cols, chans = inputs.shape
    depth = weights.shape[1]
    section_count = lax.axis_size("section")
    factor = 1.0 / math.sqrt(micros * rows * lax.axis_size("rows") * cols)
    vmem = pl.BlockSpec(memory_space=pltpu.VMEM)
    dma = pltpu.SemaphoreType.DMA
    bf16, f32 = jnp.bfloat16, jnp.float32
    outs = pl.pallas_call(
        functools.partial(kernel, section_count, factor),
        out_shape=(
            jax.ShapeDtypeStruct((micros, rows, cols, chans), bf16),
            jax.ShapeDtypeStruct((micros, rows, cols, chans), bf16),
            jax.ShapeDtypeStruct((depth, chans), f32),
        ),
        in_specs=[vmem] * 3,
        out_specs=(vmem,) * 3,
        scratch_shapes=[
            pltpu.VMEM((micros, rows + 2, cols, 3 * chans), bf16),
            pltpu.VMEM((micros, rows + 2, cols, chans), bf16),
            pltpu.VMEM((micros, rows + 2, cols, chans), f32),
            pltpu.VMEM((rows + 2, cols, 3 * chans), bf16),
            pltpu.VMEM((depth, chans), bf16),
            pltpu.VMEM((depth, chans), f32),
            pltpu.VMEM((depth, chans), bf16),
            pltpu.VMEM((depth, chans), bf16),
            dma((micros, 4)),
            dma((micros, 4)),
            dma((micros, 4)),
            dma((micros, 4)),
            dma((micros,)),
            dma((micros,)),
            dma((micros,)),
            dma((micros,)),
            dma((3,)),
            dma((3,)),
        ],
        compiler_params=pltpu.CompilerParams(
            collective_id=0, has_side_effects=True, vmem_limit_bytes=48 * 1024 * 1024
        ),
        name="relay",
    )(inputs, weights[0], cotangent)
    section_outputs, grad_inputs, weight_grads = outs
    return (section_outputs[None], grad_inputs[None], weight_grads[None])


def solution(mesh):
    placed = (
        P("groups", "rows", None, None),
        P("section", None, None),
        P("groups", "rows", None, None),
    )
    return jax.shard_map(
        on_device,
        mesh=mesh,
        in_specs=placed,
        out_specs=(
            P("section", "groups", "rows", None, None),
            P("section", "groups", "rows", None, None),
            P("section", "groups", None),
        ),
        check_vma=False,
    )
```

time: 512 us -> 145 us (0.28)
  waiting for transfers between devices: 212 us -> 0 us
  starting transfers between devices: 160 us -> 0 us
  Pallas kernels: 0 us -> 136 us
  other arithmetic: 71.4 us -> 0 us
  local copies, waits for them, and re-layouts: 39.4 us -> 7.37 us
  between operations: 14.1 us -> 0.66 us
  matrix products: 9.47 us -> 0 us
    ppermute x66 -> x0, waiting for transfers between devices: 192 us -> none  [the longest x22 164 us: shifted(): return lax.ppermute(block, axis, route)]
    ppermute x66 -> x0, starting transfers between devices: 160 us -> none  [the longest x22 70.6 us: shifted(): return lax.ppermute(block, axis, route)]
    pallas_call x0 -> x1, Pallas kernels: none -> 136 us  [on_device(): pl.pallas_call(functools.partial(kernel, section_count, factor), out_shap...]
    add x11 -> x0, other arithmetic: 35.6 us -> none  [backward_tick(): grad_total = grad_total + increment]
    psum x1 -> x0, waiting for transfers between devices: 19.5 us -> none  [on_device(): lax.psum(grad_total.astype(jnp.bfloat16), 'rows').astype(jnp.float32)]
    dynamic_update_slice x15 -> x0, other arithmetic: 11.9 us -> none  [the longest x11 8.44 us: backward_tick(): lax.dynamic_update_index_in_dim(kept_grads, jnp.where(active, passed, pre...]
    select_n x11 -> x0, other arithmetic: 10.8 us -> none  [forward_tick(): current = jnp.where(section_pos == 0, source, arriving)]
    dynamic_slice x11 -> x0, local copies, waits for them, and re-layouts: 10.7 us -> none  [backward_tick(): previous = lax.dynamic_index_in_dim(kept_grads, clamped, 0, keepdims=False)]
  transfers between devices with their start and end apart: 67 -> 0, of which waited for: 45 -> 0; matrix products, arithmetic and copies ran while one was open for 11% -> 0% of each run, Pallas kernels for 0% -> 0%
where the time goes in v1:
time: 145 us; the launch traced here: 144 us
  Pallas kernels  136 us (94%)
  local copies, waits for them, and re-layouts  7.37 us (5%)
    pallas_call x1, Pallas kernels, on_device(): pl.pallas_call(functools.partial(kernel, section_count, factor), out_shap...  136 us
    unnamed x11, local copies, waits for them, and re-layouts  7.37 us

profile of v1, /device:TPU:1, one launch (start us, length us, event | category | flops | bytes accessed | tf_op | source)
XLA Modules:
  0.0 144.3 jit_solution(562664024724594101)
XLA Ops:
  0.6 0.0 copy-start
  0.6 1.3 copy-done
  1.9 0.0 copy-start.1
  1.9 1.2 copy-done.1
  3.1 0.0 copy-start.2
  3.1 1.2 copy-done.2
  4.4 136.3 %relay.1 = (bf16[4,8,64,256]{3,2,1,0:T(8,128)(2,1)S(1)}, bf16[4,8,64,256]{3,2,1,0:T(8,128)(2,1)S(1)}, f32[2304,256]{1,0:T(8,128)}) custom-call(bf16[4,8,64,256]{3,2,1,0:T(8,128)(2,1)S(1)} %copy-done.1, bf16[2304,256]{1,0:T(8,128)(2,1)S(1)} %bitcast.4, bf16[4,8,64,256]{3,2,1,0:T(8,128)(2,1)S(1)} %copy-done.2), custom_call_target="tpu_custom_call" | custom-call | tf_op jit(solution)/shard_map/relay/pallas_call | solution.py:356
  140.6 0.0 copy-start.3
  140.7 1.0 copy.9
  141.6 1.0 copy.10
  142.6 0.3 copy-done.3
  142.9 1.4 copy.11
Async XLA Ops:
  0.6 1.3 copy-start
  1.9 1.2 copy-start.1
  3.1 1.2 copy-start.2
  140.6 2.3 %copy-start.3 = (f32[2304,256]{1,0:T(8,128)S(1)}, f32[2304,256]{1,0:T(8,128)}, u32[]{:S(2)}) copy-start(f32[2304,256]{1,0:T(8,128)} %get-tuple-element.8) | copy-start | bytes 7077892

commit v2 on v1

--- a/solution.py
+++ b/solution.py
@@ -11,6 +11,7 @@
 MESH = pl.DeviceIdType.MESH
 tanh_scale = 0.7978845608028654
 cubic_term = 0.044715
+PARTS = 4
 
 
 def column_shifts(values):
@@ -29,11 +30,12 @@
     section_count,
     factor,
     in_ref,
-    w_ref,
+    w_hbm,
     cot_ref,
     out_ref,
     grad_ref,
     wgrad_ref,
+    w_ref,
     x3,
     u,
     slope,
@@ -52,9 +54,12 @@
     recv_s,
     send_w,
     recv_w,
+    sem_in,
+    sem_wt,
 ):
     micros, rows, cols, chans = in_ref.shape
-    half = rows // 2
+    step = rows // PARTS
+    last_part = PARTS - 1
     mid = pl.ds(chans, chans)
     s = lax.axis_index("section")
     r = lax.axis_index("rows")
@@ -67,6 +72,30 @@
     halo = (1 - r) * (rows + 1)
     other_halo = r * (rows + 1)
 
+    weight_copy = pltpu.make_async_copy(w_hbm, w_ref, sem_wt)
+    weight_copy.start()
+
+    def own_input(m):
+        return pltpu.make_async_copy(in_ref.at[m], x3.at[m, pl.ds(1, rows), :, mid], sem_in.at[m])
+
+    def own_cotangent(m):
+        return pltpu.make_async_copy(cot_ref.at[m], u.at[m, pl.ds(1, rows)], sem_in.at[m])
+
+    def each_micro(action):
+        def body(m, carry):
+            action(m)
+            return carry
+
+        lax.fori_loop(0, micros, body, 0)
+
+    @pl.when(is_first)
+    def _():
+        each_micro(lambda m: own_input(m).start())
+
+    @pl.when(is_last)
+    def _():
+        each_micro(lambda m: own_cotangent(m).start())
+
     barrier = pltpu.get_barrier_semaphore()
     pl.semaphore_signal(barrier, inc=1, device_id={"rows": other}, device_id_type=MESH)
 
@@ -92,7 +121,7 @@
             src_ref=in_ref.at[m, pl.ds(edge, 1)],
             dst_ref=x3.at[m, pl.ds(dst_row, 1), :, mid],
             send_sem=send_i.at[m],
-            recv_sem=recv_f.at[m, 2],
+            recv_sem=recv_f.at[m, 2 * PARTS - 1],
             device_id={"rows": other},
             device_id_type=MESH,
         )
@@ -102,7 +131,7 @@
             src_ref=cot_ref.at[m, pl.ds(edge, 1)],
             dst_ref=u.at[m, pl.ds(dst_row, 1)],
             send_sem=send_c.at[m],
-            recv_sem=recv_b.at[m, 2],
+            recv_sem=recv_b.at[m, 2 * PARTS - 1],
             device_id={"rows": other},
             device_id_type=MESH,
         )
@@ -117,49 +146,51 @@
             device_id_type=MESH,
         )
 
-    starts = (r * half, half - r, edge, (1 - r) * (half + 1))
-    counts = (half, 1, 1, half - 1)
+    def run_start(q, n):
+        return q + r * (rows - 2 * q - n)
+
+    pieces = [(0, step)]
+    pieces += [(k * step + 1, step - 1) for k in range(1, PARTS)]
+    pieces += [(k * step, 1) for k in range(1, PARTS)]
+    pieces += [(rows - 1, 1)]
+    middle = 2 * PARTS - 1
+    needs = [(k, PARTS + k if k < last_part else middle) for k in range(PARTS)]
+    gives = [(0,)] + [(PARTS - 1 + k, k) for k in range(1, last_part)]
+    gives += [(PARTS - 1 + last_part, middle, last_part)]
 
     def forward_piece(m, p, halo_row):
-        start, count = starts[p], counts[p]
-        where = halo_row if p == 2 else start + 1
+        q, count = pieces[p]
+        start = run_start(q, count)
+        where = halo_row if p == middle else start + 1
         return pltpu.make_async_remote_copy(
             src_ref=out_ref.at[m, pl.ds(start, count)],
             dst_ref=x3.at[m, pl.ds(where, count), :, mid],
             send_sem=send_f.at[m, p],
             recv_sem=recv_f.at[m, p],
-            device_id={"section": jnp.minimum(s + 1, last), "rows": other if p == 2 else r},
+            device_id={"section": jnp.minimum(s + 1, last), "rows": other if p == middle else r},
             device_id_type=MESH,
         )
 
     def backward_piece(m, p, halo_row):
-        start, count = starts[p], counts[p]
-        where = halo_row if p == 2 else start + 1
+        q, count = pieces[p]
+        start = run_start(q, count)
+        where = halo_row if p == middle else start + 1
         return pltpu.make_async_remote_copy(
             src_ref=grad_ref.at[m, pl.ds(start, count)],
             dst_ref=u.at[m, pl.ds(where, count)],
             send_sem=send_b.at[m, p],
             recv_sem=recv_b.at[m, p],
-            device_id={"section": jnp.maximum(s - 1, 0), "rows": other if p == 2 else r},
+            device_id={"section": jnp.maximum(s - 1, 0), "rows": other if p == middle else r},
             device_id_type=MESH,
         )
 
     @pl.when(is_first)
     def _():
-        def start(m, carry):
-            first_halo(m, other_halo).start()
-            return carry
-
-        lax.fori_loop(0, micros, start, 0)
+        each_micro(lambda m: first_halo(m, other_halo).start())
 
     @pl.when(is_last)
     def _():
-        def start(m, carry):
-            last_halo(m, other_halo).start()
-            u[m, pl.ds(1, rows)] = cot_ref[m]
-            return carry
-
-        lax.fori_loop(0, micros, start, 0)
+        each_micro(lambda m: last_halo(m, other_halo).start())
 
     blank = jnp.zeros((1, cols, 3 * chans), jnp.bfloat16)
 
@@ -170,6 +201,8 @@
     lax.fori_loop(0, micros, clear, 0)
     g3[pl.ds(other_halo, 1)] = blank
 
+    weight_copy.wait()
+
     def transpose_weights():
         for k in range(9):
             wt[pl.ds((8 - k) * chans, chans), :] = w_ref[pl.ds(k * chans, chans), :].T
@@ -178,15 +211,13 @@
     def _():
         transpose_weights()
 
-    new_starts = (1 + r * (half - 1), (1 - r) * (half + 2))
-    new_counts = (half + 1, rows - half)
-    half_starts = (r * half, (1 - r) * half)
+    fresh_runs = [(0, step + 1)] + [(k * step + 1, step) for k in range(1, PARTS)]
 
     def conv(field, kern, start):
         total = None
         for a in range(3):
             part = jnp.dot(
-                field[pl.ds(start + a, half)].reshape(half * cols, 3 * chans),
+                field[pl.ds(start + a, step)].reshape(step * cols, 3 * chans),
                 kern[pl.ds(a * 3 * chans, 3 * chans), :],
                 preferred_element_type=jnp.float32,
             )
@@ -196,35 +227,36 @@
     def forward(m):
         @pl.when(is_first)
         def _():
-            x3[m, pl.ds(1, rows), :, mid] = in_ref[m]
-
-        for k in range(2):
+            own_input(m).wait()
+
+        for k in range(PARTS):
             @pl.when(s > 0)
             def _():
-                for p in ((0, 1), (3,))[k]:
-                    forward_piece(m, p, halo).wait_recv()
-
-            if k == 1:
-                forward_piece(m, 2, halo).wait_recv()
-            fresh = pl.ds(new_starts[k], new_counts[k])
+                for p in needs[k]:
+                    if p != middle:
+                        forward_piece(m, p, halo).wait_recv()
+
+            if k == last_part:
+                forward_piece(m, middle, halo).wait_recv()
+            fresh = pl.ds(run_start(*fresh_runs[k]) + 1, fresh_runs[k][1])
             left, right = column_shifts(x3[m, fresh, :, mid].astype(jnp.float32))
             x3[m, fresh, :, pl.ds(0, chans)] = left
             x3[m, fresh, :, pl.ds(2 * chans, chans)] = right
-            start = half_starts[k]
+            start = run_start(k * step, step)
             pre = conv(x3.at[m], w_ref, start)
             curved = jnp.tanh(tanh_scale * (pre + cubic_term * pre * pre * pre))
             value = 0.5 * pre * (1.0 + curved)
-            out_ref[m, pl.ds(start, half)] = value.astype(jnp.bfloat16).reshape(half, cols, chans)
+            out_ref[m, pl.ds(start, step)] = value.astype(jnp.bfloat16).reshape(step, cols, chans)
 
             @pl.when(s < last)
             def _():
-                for p in ((0,), (1, 2, 3))[k]:
+                for p in gives[k]:
                     forward_piece(m, p, other_halo).start()
 
             steep = 0.5 * (1.0 + curved) + 0.5 * pre * (1.0 - curved * curved) * tanh_scale * (
                 1.0 + 3.0 * cubic_term * pre * pre
             )
-            slope[m, pl.ds(start + 1, half)] = steep.reshape(half, cols, chans)
+            slope[m, pl.ds(start + 1, step)] = steep.reshape(step, cols, chans)
         slope_halo(m, other_halo).start()
 
     def kernel_term(m, a):
@@ -236,28 +268,33 @@
         )
 
     def backward(m):
-        for k in range(2):
+        @pl.when(is_last)
+        def _():
+            own_cotangent(m).wait()
+
+        for k in range(PARTS):
             @pl.when(s < last)
             def _():
-                for p in ((0, 1), (3,))[k]:
-                    backward_piece(m, p, halo).wait_recv()
-
-            if k == 1:
-                backward_piece(m, 2, halo).wait_recv()
+                for p in needs[k]:
+                    if p != middle:
+                        backward_piece(m, p, halo).wait_recv()
+
+            if k == last_part:
+                backward_piece(m, middle, halo).wait_recv()
                 slope_halo(m, halo).wait_recv()
-            fresh = pl.ds(new_starts[k], new_counts[k])
+            fresh = pl.ds(run_start(*fresh_runs[k]) + 1, fresh_runs[k][1])
             local = (u[m, fresh].astype(jnp.float32) * slope[m, fresh]).astype(jnp.bfloat16)
             left, right = column_shifts(local.astype(jnp.float32))
             g3[fresh, :, pl.ds(0, chans)] = left
             g3[fresh, :, mid] = local
             g3[fresh, :, pl.ds(2 * chans, chans)] = right
-            start = half_starts[k]
+            start = run_start(k * step, step)
             passed = conv(g3, wt, start)
-            grad_ref[m, pl.ds(start, half)] = passed.astype(jnp.bfloat16).reshape(half, cols, chans)
+            grad_ref[m, pl.ds(start, step)] = passed.astype(jnp.bfloat16).reshape(step, cols, chans)
 
             @pl.when(s > 0)
             def _():
-                for p in ((0,), (1, 2, 3))[k]:
+                for p in gives[k]:
                     backward_piece(m, p, other_halo).start()
 
         @pl.when(m == 0)
@@ -322,12 +359,12 @@
 
         @pl.when(s < last)
         def _():
-            for p in range(4):
+            for p in range(2 * PARTS):
                 forward_piece(m, p, other_halo).wait_send()
 
         @pl.when(s > 0)
         def _():
-            for p in range(4):
+            for p in range(2 * PARTS):
                 backward_piece(m, p, other_halo).wait_send()
 
         @pl.when(is_first)
@@ -360,9 +397,10 @@
             jax.ShapeDtypeStruct((micros, rows, cols, chans), bf16),
             jax.ShapeDtypeStruct((depth, chans), f32),
         ),
-        in_specs=[vmem] * 3,
+        in_specs=[pl.BlockSpec(memory_space=pl.ANY)] * 3,
         out_specs=(vmem,) * 3,
         scratch_shapes=[
+            pltpu.VMEM((depth, chans), bf16),
             pltpu.VMEM((micros, rows + 2, cols, 3 * chans), bf16),
             pltpu.VMEM((micros, rows + 2, cols, chans), bf16),
             pltpu.VMEM((micros, rows + 2, cols, chans), f32),
@@ -371,16 +409,18 @@
             pltpu.VMEM((depth, chans), f32),
             pltpu.VMEM((depth, chans), bf16),
             pltpu.VMEM((depth, chans), bf16),
-            dma((micros, 4)),
-            dma((micros, 4)),
-            dma((micros, 4)),
-            dma((micros, 4)),
+            dma((micros, 2 * PARTS)),
+            dma((micros, 2 * PARTS)),
+            dma((micros, 2 * PARTS)),
+            dma((micros, 2 * PARTS)),
             dma((micros,)),
             dma((micros,)),
             dma((micros,)),
             dma((micros,)),
             dma((3,)),
             dma((3,)),
+            dma((micros,)),
+            dma,
         ],
         compiler_params=pltpu.CompilerParams(
             collective_id=0, has_side_effects=True, vmem_limit_bytes=48 * 1024 * 1024

time: 145 us -> 129 us (0.89)
  Pallas kernels: 136 us -> 120 us
    pallas_call x1, Pallas kernels: 136 us -> 120 us  [on_device(): pl.pallas_call(functools.partial(kernel, section_count, factor), out_shap...]
where the time goes in v2:
time: 129 us
  Pallas kernels  120 us (93%)
  local copies, waits for them, and re-layouts  7.37 us (6%)
    pallas_call x1, Pallas kernels, on_device(): pl.pallas_call(functools.partial(kernel, section_count, factor), out_shap...  120 us
    unnamed x11, local copies, waits for them, and re-layouts  7.37 us

profile of v2, /device:TPU:1, one launch (start us, length us, event | category | flops | bytes accessed | tf_op | source)
XLA Modules:
  0.0 128.5 jit_solution(8469441438950415760)
XLA Ops:
  0.6 0.0 copy-start
  0.6 1.3 copy-done
  1.9 0.0 copy-start.1
  1.9 1.2 copy-done.1
  3.1 0.0 copy-start.2
  3.1 1.2 copy-done.2
  4.4 120.5 %relay.1 = (bf16[4,8,64,256]{3,2,1,0:T(8,128)(2,1)S(1)}, bf16[4,8,64,256]{3,2,1,0:T(8,128)(2,1)S(1)}, f32[2304,256]{1,0:T(8,128)}) custom-call(bf16[4,8,64,256]{3,2,1,0:T(8,128)(2,1)S(1)} %copy-done.1, bf16[2304,256]{1,0:T(8,128)(2,1)S(1)} %bitcast.4, bf16[4,8,64,256]{3,2,1,0:T(8,128)(2,1)S(1)} %copy-done.2), custom_call_target="tpu_custom_call" | custom-call | tf_op jit(solution)/shard_map/relay/pallas_call | solution.py:393
  124.8 0.0 copy-start.3
  124.9 1.0 copy.9
  125.8 1.0 copy.10
  126.8 0.3 copy-done.3
  127.1 1.4 %copy.11 = f32[1,2304,256]{2,1,0:T(8,128)} copy(f32[1,2304,256]{2,1,0:T(8,128)S(1)} %bitcast.7) | data formatting | bytes 4718592
Async XLA Ops:
  0.6 1.3 copy-start
  1.9 1.2 copy-start.1
  3.1 1.2 copy-start.2
  124.8 2.3 %copy-start.3 = (f32[2304,256]{1,0:T(8,128)S(1)}, f32[2304,256]{1,0:T(8,128)}, u32[]{:S(2)}) copy-start(f32[2304,256]{1,0:T(8,128)} %get-tuple-element.8) | copy-start | bytes 7077892

commit v3 on v2

--- a/solution.py
+++ b/solution.py
@@ -28,13 +28,13 @@
 
 def kernel(
     section_count,
-    factor,
     in_ref,
     w_hbm,
     cot_ref,
     out_ref,
     grad_ref,
-    wgrad_ref,
+    wsend,
+    wrecv,
     w_ref,
     x3,
     u,
@@ -42,8 +42,6 @@
     g3,
     wt,
     acc,
-    wsend,
-    wrecv,
     send_f,
     recv_f,
     send_b,
@@ -348,11 +346,7 @@
         wsend[block, :] = total.astype(jnp.bfloat16)
         kernel_copy(a).start()
     for a in range(3):
-        block = pl.ds(a * 3 * chans, 3 * chans)
         kernel_copy(a).wait_recv()
-        wgrad_ref[block, :] = (
-            wsend[block, :].astype(jnp.float32) + wrecv[block, :].astype(jnp.float32)
-        ) * factor
 
     def finish(m, carry):
         slope_halo(m, other_halo).wait_send()
@@ -391,14 +385,15 @@
     dma = pltpu.SemaphoreType.DMA
     bf16, f32 = jnp.bfloat16, jnp.float32
     outs = pl.pallas_call(
-        functools.partial(kernel, section_count, factor),
+        functools.partial(kernel, section_count),
         out_shape=(
             jax.ShapeDtypeStruct((micros, rows, cols, chans), bf16),
             jax.ShapeDtypeStruct((micros, rows, cols, chans), bf16),
-            jax.ShapeDtypeStruct((depth, chans), f32),
+            jax.ShapeDtypeStruct((depth, chans), bf16),
+            jax.ShapeDtypeStruct((depth, chans), bf16),
         ),
         in_specs=[pl.BlockSpec(memory_space=pl.ANY)] * 3,
-        out_specs=(vmem,) * 3,
+        out_specs=(vmem,) * 4,
         scratch_shapes=[
             pltpu.VMEM((depth, chans), bf16),
             pltpu.VMEM((micros, rows + 2, cols, 3 * chans), bf16),
@@ -407,8 +402,6 @@
             pltpu.VMEM((rows + 2, cols, 3 * chans), bf16),
             pltpu.VMEM((depth, chans), bf16),
             pltpu.VMEM((depth, chans), f32),
-            pltpu.VMEM((depth, chans), bf16),
-            pltpu.VMEM((depth, chans), bf16),
             dma((micros, 2 * PARTS)),
             dma((micros, 2 * PARTS)),
             dma((micros, 2 * PARTS)),
@@ -427,7 +420,8 @@
         ),
         name="relay",
     )(inputs, weights[0], cotangent)
-    section_outputs, grad_inputs, weight_grads = outs
+    section_outputs, grad_inputs, mine, theirs = outs
+    weight_grads = (mine.astype(f32) + theirs.astype(f32)) * factor
     return (section_outputs[None], grad_inputs[None], weight_grads[None])
 
 

time: 129 us -> 128 us (level)
  local copies, waits for them, and re-layouts: 7.37 us -> 4.38 us
  other arithmetic: 0 us -> 2.98 us
    unnamed x11 -> x6, local copies, waits for them, and re-layouts: 7.37 us -> 4.38 us
    broadcast_in_dim x0 -> x1, other arithmetic: none -> 2.98 us  [on_device(): return (section_outputs[None], grad_inputs[None], weight_grads[None])]
where the time goes in v3:
time: 128 us
  Pallas kernels  120 us (94%)
  local copies, waits for them, and re-layouts  4.38 us (3%)
  other arithmetic  2.98 us (2%)
    pallas_call x1, Pallas kernels, on_device(): pl.pallas_call(functools.partial(kernel, section_count), out_shape=(jax.S...  120 us
    unnamed x6, local copies, waits for them, and re-layouts  4.38 us
    broadcast_in_dim x1, other arithmetic, on_device(): return (section_outputs[None], grad_inputs[None], weight_grads[None])  2.98 us

profile of v3, /device:TPU:1, one launch (start us, length us, event | category | flops | bytes accessed | tf_op | source)
XLA Modules:
  0.0 127.7 jit_solution(1549308024347607011)
XLA Ops:
  0.6 0.0 copy-start
  0.6 1.2 copy-done
  1.9 0.0 copy-start.1
  1.9 1.2 copy-done.1
  3.1 119.7 %relay.1 = (bf16[4,8,64,256]{3,2,1,0:T(8,128)(2,1)S(1)}, bf16[4,8,64,256]{3,2,1,0:T(8,128)(2,1)S(1)}, bf16[2304,256]{1,0:T(8,128)(2,1)S(1)}, bf16[2304,256]{1,0:T(8,128)(2,1)}) custom-call(bf16[4,8,64,256]{3,2,1,0:T(8,128)(2,1)S(1)} %copy-done, bf16[2304,256]{1,0:T(8,128)(2,1)} %bitcast.7, bf16[4,8,64,256]{3,2,1,0:T(8,128)(2,1)S(1)} %copy-done.1), custom_call_target="tpu_custom_call" | custom-call | tf_op jit(solution)/shard_map/relay/pallas_call | solution.py:387
  122.8 3.0 %multiply_bitcast_fusion = f32[1,2304,256]{2,1,0:T(8,128)} fusion(bf16[2304,256]{1,0:T(8,128)(2,1)} %get-tuple-element.10, bf16[2304,256]{1,0:T(8,128)(2,1)S(1)} %get-tuple-element.9), kind=kLoop, calls=%fused_computation | loop fusion | flops 2359296 | bytes 4718592 | tf_op jit(solution)/shard_map/broadcast_in_dim | solution.py:425
  125.8 1.0 copy.8
  126.8 1.0 copy.9
Async XLA Ops:
  0.6 1.2 copy-start
  1.9 1.2 copy-start.1
